TPU v7x, 32 devices: a whole 2x2x4 slice. The times are simulated.
32 devices in a mesh: grp: 2 (over y), seq: 4 (over z), col: 4 (over x, core).
Axes of the slice: x: 2, y: 2, z: 4, core: 2. Of those that a mesh axis runs over, the one named last changes fastest.
Arguments:
- tokens: bfloat16 [4096, 4608], P(('grp', 'seq'), 'col'), parts along dimension 0, may hold values from -14 to 14
- norm_gain: float32 [4608], replicated, may hold values from 0.5 to 1.5
- query_weight: bfloat16 [4608, 2048], P('seq', 'col'), may hold values from -1 to 1
- key_weight: bfloat16 [4608, 1024], P('seq', 'col'), may hold values from -1 to 1
- value_weight: bfloat16 [4608, 1024], P('seq', 'col'), may hold values from -0.09375 to 0.09375
- out_weight: bfloat16 [2048, 4608], P('seq', 'col'), may hold values from -1 to 1
- positions: int32 [4096], P(('grp', 'seq')), parts along dimension 0, may hold values from 0 to 2047, as said below
Outputs:
- block_out: bfloat16 [4096, 4608], P(('grp', 'seq'), 'col'), parts along dimension 0
There are 2 independent parts, one for each index of `grp`. A program takes and returns all parts, laid end to end along the dimension named above; an argument that names none is the same for every part. Nothing has to cross between parts.
Inputs may be any that keep to these rules, and one draw needn't show every extreme that they name: Within a document positions rise by one from token to token. Exactly one document starts inside the slab, at a token of its middle half, where positions restart at 0; the document before it ends at position 2047.
All inputs are finite; a program needn't handle non-finite values.
Results may differ from a plain program's by a relative error of at most 0.012.
The roundings to bfloat16 on the way count: a program that leaves them out, or rounds other values in their place, can miss the bound.
Values may be sent and summed in bfloat16 or wider, within the bound.
A program may use at most 64 MiB of HBM per device.

v0:
```python
import jax
import jax.numpy as jnp
from jax import lax
from jax.sharding import PartitionSpec as P

KVH = 8
HD = 128
WIN = 4096
score_scale = 1.0 / 12.0
rope_base = 10000.0


def passed_along(block, axis, distance):
    devices = range(lax.axis_size(axis))
    route = [(i - distance, i) for i in devices if i - distance in devices]
    return lax.ppermute(block, axis, route)


def rms_norm(values_in, norm_gain):
    floats = values_in.astype(jnp.float32)
    square_mean = jnp.mean(floats * floats, axis=-1, keepdims=True)
    return (floats * lax.rsqrt(square_mean + 1e-06) * norm_gain).astype(jnp.bfloat16)


def rotate(heads_in, places):
    width = heads_in.shape[-1]
    half = width // 2
    inverse = jnp.exp(-jnp.log(rope_base) * jnp.arange(half, dtype=jnp.float32) * (2.0 / width))
    angle = places.astype(jnp.float32)[:, None] * inverse[None, :]
    cosine = jnp.cos(angle)[:, None, :]
    sine = jnp.sin(angle)[:, None, :]
    lower = heads_in[..., :half]
    upper = heads_in[..., half:]
    return jnp.concatenate([lower * cosine - upper * sine, upper * cosine + lower * sine], axis=-1)


def per_device(tokens, norm_gain, query_weight, key_weight, value_weight, out_weight, positions):
    tok_rows = tokens.shape[0]
    col_count = lax.axis_size("col")
    seq_count = lax.axis_size("seq")
    seq_index = lax.axis_index("seq")
    kv_local = KVH // col_count
    whole = lax.all_gather(tokens, "col", axis=1, tiled=True)
    normed = rms_norm(whole, norm_gain)
    all_places = lax.all_gather(positions, "seq", axis=0, tiled=True)
    pieces = (
        lax.all_gather(query_weight, "seq", axis=0, tiled=True),
        lax.all_gather(key_weight, "seq", axis=0, tiled=True),
        lax.all_gather(value_weight, "seq", axis=0, tiled=True),
    )
    columns = normed
    query_raw, key_raw, value_raw = tuple(
        (jnp.dot(columns, piece, preferred_element_type=jnp.float32) for piece in pieces)
    )
    queries = (
        rotate(query_raw.reshape(tok_rows, 2 * kv_local, HD), positions)
        .astype(jnp.bfloat16)
        .reshape(tok_rows, kv_local, 2, HD)
    )
    keys = (
        rotate(key_raw.reshape(tok_rows, kv_local, HD), positions)
        .astype(jnp.bfloat16)
        .reshape(tok_rows, kv_local * HD)
    )
    values = value_raw.astype(jnp.bfloat16)
    packed = jnp.stack([keys, values])
    reach = min(WIN // tok_rows, seq_count - 1)
    blocks = [packed]
    current = packed
    for step in range(reach):
        current = passed_along(current, "seq", 1)
        blocks.insert(0, current)
    window = jnp.concatenate(blocks, axis=1)
    span = (reach + 1) * tok_rows
    places_pad = jnp.concatenate([jnp.zeros((reach * tok_rows,), jnp.int32), all_places], axis=0)
    key_places = lax.dynamic_slice_in_dim(places_pad, seq_index * tok_rows, span, 0)
    key_index = (seq_index - reach) * tok_rows + jnp.arange(span, dtype=jnp.int32)
    query_index = seq_index * tok_rows + jnp.arange(tok_rows, dtype=jnp.int32)
    group = 1
    for candidate in range(1, reach + 2):
        if (reach + 1) % candidate == 0 and candidate * tok_rows <= max(512, tok_rows):
            group = candidate
    key_rows = group * tok_rows
    key_blocks = span // key_rows
    keys_blocked = window[0].reshape(key_blocks, key_rows, kv_local, HD)[::-1]
    values_blocked = window[1].reshape(key_blocks, key_rows, kv_local, HD)[::-1]
    places_blocked = key_places.reshape(key_blocks, key_rows)[::-1]
    index_blocked = key_index.reshape(key_blocks, key_rows)[::-1]

    def attend(carry, block):
        largest, total, summed = carry
        key_part, value_part, place_part, index_part = block
        scores = (
            jnp.einsum("qgeh,kgh->qgek", queries, key_part, preferred_element_type=jnp.float32)
            * score_scale
        )
        distance = query_index[:, None] - index_part[None, :]
        visible = (index_part[None, :] >= 0) & (distance >= 0) & (distance < WIN)
        visible = visible & (positions[:, None] - place_part[None, :] == distance)
        scores = jnp.where(visible[:, None, None, :], scores, -1e30)
        newest = jnp.maximum(largest, jnp.max(scores, axis=-1))
        factor = jnp.exp(largest - newest)
        weights = jnp.exp(scores - newest[..., None])
        total = total * factor + jnp.sum(weights, axis=-1)
        summed = summed * factor[..., None] + jnp.einsum(
            "qgek,kgh->qgeh",
            weights.astype(jnp.bfloat16),
            value_part,
            preferred_element_type=jnp.float32,
        )
        return ((newest, total, summed), None)

    start_state = (
        jnp.full((tok_rows, kv_local, 2), -1e30, jnp.float32),
        jnp.zeros((tok_rows, kv_local, 2), jnp.float32),
        jnp.zeros((tok_rows, kv_local, 2, HD), jnp.float32),
    )
    final_state, unused = lax.scan(
        attend, start_state, (keys_blocked, values_blocked, places_blocked, index_blocked)
    )
    attended = (
        (final_state[2] / final_state[1][..., None])
        .astype(jnp.bfloat16)
        .reshape(tok_rows, 2 * kv_local * HD)
    )
    mixed = lax.all_gather(attended, "col", axis=1, tiled=True)
    columns = mixed
    projected = jnp.dot(
        columns,
        lax.all_gather(out_weight, "seq", axis=0, tiled=True),
        preferred_element_type=jnp.float32,
    )
    return (tokens.astype(jnp.float32) + projected).astype(jnp.bfloat16)


def solution(mesh):
    return jax.shard_map(
        per_device,
        mesh=mesh,
        in_specs=(
            P(("grp", "seq"), "col"),
            P(),
            P("seq", "col"),
            P("seq", "col"),
            P("seq", "col"),
            P("seq", "col"),
            P(("grp", "seq")),
        ),
        out_specs=P(("grp", "seq"), "col"),
        check_vma=False,
    )
```

profile of v0, /device:TPU:0, one launch (start us, length us, event | category | flops | bytes accessed | tf_op | source)
XLA Modules:
  0.0 397.1 jit_solution(13647404061947721689)
XLA Ops:
  10.6 38.5 %all-gather.8.cloned.1.call-done = bf16[512,4608]{1,0:T(8,128)(2,1)} async-done(((bf16[512,1152]{1,0:T(8,128)(2,1)}), bf16[512,4608]{1,0:T(8,128)(2,1)}) %all-gather.8.cloned.1.call-update) | async-done | bytes 4718608 | tf_op jit(solution)/shard_map/all_gather | solution.py:43
  49.1 3.3 fusion.31
  52.4 48.7 %all-gather.10.cloned.1.call-done = bf16[4608,256]{1,0:T(8,128)(2,1)} async-done(((bf16[1152,256]{1,0:T(8,128)(2,1)}), bf16[4608,256]{1,0:T(8,128)(2,1)}) %all-gather.10.cloned.1.call-update) | async-done | bytes 2359312 | tf_op jit(solution)/shard_map/all_gather | solution.py:48
  101.2 4.8 %fusion.39 = f32[512,256]{0,1:T(8,128)S(1)} fusion(bf16[4608,256]{1,0:T(8,128)(2,1)} %all-gather.10.cloned.1.call-done, bf16[512,4608]{1,0:T(8,128)(2,1)} %all-gather.8.cloned.1.call-done, f32[4608]{0:T(1024)S(1)} %copy-done.5, f32[512]{0:T(512)S(1)} %add_rsqrt_fusion), kind=kOutput, calls=%fused_computation.64 | convolution fusion | flops 1217396736 | bytes 7622656 | tf_op jit(solution)/shard_map/dot_general | solution.py:53
  106.3 45.8 %all-gather.12.cloned.1.call-done = bf16[4608,256]{1,0:T(8,128)(2,1)} async-done(((bf16[1152,256]{1,0:T(8,128)(2,1)}), bf16[4608,256]{1,0:T(8,128)(2,1)}) %all-gather.12.cloned.1.call-update) | async-done | bytes 2359312 | tf_op jit(solution)/shard_map/all_gather | solution.py:49
  152.1 4.6 %fusion.35 = bf16[1,512,256]{2,1,0:T(8,128)(2,1)S(1)} fusion(bf16[4608,256]{1,0:T(8,128)(2,1)} %all-gather.12.cloned.1.call-done, bf16[512,4608]{1,0:T(8,128)(2,1)} %all-gather.8.cloned.1.call-done, f32[4608]{0:T(1024)S(1)} %copy-done.5, f32[512]{0:T(512)S(1)} %add_rsqrt_fusion), kind=kOutput, calls=%fused_computation.47 | convolution fusion | flops 1217527808 | bytes 7360512 | tf_op jit(solution)/shard_map/dot_general | solution.py:53
  156.7 1.8 collective-permute-start
  158.5 20.3 %collective-permute-done = bf16[2,512,256]{2,1,0:T(8,128)(2,1)S(1)} collective-permute-done((bf16[2,512,256]{2,1,0:T(8,128)(2,1)S(1)}, bf16[2,512,256]{2,1,0:T(8,128)(2,1)S(1)}, u32[]{:S(2)}, u32[]{:S(2)}) %collective-permute-start) | collective-permute-done | bytes 524320 | tf_op jit(solution)/shard_map/ppermute | solution.py:16
  178.9 13.4 %collective-permute-start.1 = (bf16[2,512,256]{2,1,0:T(8,128)(2,1)S(1)}, bf16[2,512,256]{2,1,0:T(8,128)(2,1)S(1)}, u32[]{:S(2)}, u32[]{:S(2)}) collective-permute-start(bf16[2,512,256]{2,1,0:T(8,128)(2,1)S(1)} %collective-permute-done), channel_id=1, source_target_pairs={{0,4},{4,8},{8,12},{1,5},{5,9},{9,13},{2,6},{6,10},{10,14},{3,7},{... | collective-permute-start | bytes 1572872 | tf_op jit(solution)/shard_map/ppermute | solution.py:16
  192.4 45.2 %all-gather = s32[4,1,512]{2,1,0:T(1,128)S(1)} all-gather(s32[1,1,512]{2,1,0:T(1,128)S(1)} %bitcast.75), channel_id=1, replica_groups=mesh['grp'=2,'seq'=4,'col'=4] {'seq'}, dimensions={0}, use_global_device_ids=true | all-gather | bytes 10240 | tf_op jit(solution)/shard_map/all_gather | solution.py:45
  239.6 2.1 collective-permute-start.2
  241.8 26.4 %all-gather.14.cloned.1.call-done = bf16[4608,512]{1,0:T(8,128)(2,1)} async-done(((bf16[1152,512]{1,0:T(8,128)(2,1)}), bf16[4608,512]{1,0:T(8,128)(2,1)}) %all-gather.14.cloned.1.call-update) | async-done | bytes 4718608 | tf_op jit(solution)/shard_map/all_gather | solution.py:47
  268.2 6.9 %fusion.36 = f32[512,512]{0,1:T(8,128)S(1)} fusion(bf16[4608,512]{1,0:T(8,128)(2,1)} %all-gather.14.cloned.1.call-done, bf16[512,4608]{1,0:T(8,128)(2,1)} %all-gather.8.cloned.1.call-done, f32[4608]{0:T(1024)S(1)} %copy-done.5, f32[512]{0:T(512)S(1)} %add_rsqrt_fusion), kind=kOutput, calls=%fused_computation.63 | convolution fusion | flops 2425356288 | bytes 10506240 | tf_op jit(solution)/shard_map/dot_general | solution.py:53
  280.6 2.0 copy.19
  282.6 2.2 rev.15
  284.8 47.7 %while.15 = (s32[]{:T(128)}, f32[512,2,2]{0,2,1:T(2,128)S(1)}, f32[512,2,2]{0,2,1:T(2,128)S(1)}, f32[512,2,2,128]{0,3,2,1:T(8,128)}, s32[4,512]{1,0:T(4,128)}, /...) while((s32[]{:T(128)}, f32[512,2,2]{0,2,1:T(2,128)S(1)}, ...), condition=%wide.region_4.5_spmd.clone, body=%wide.region_1.4_spmd.clone.sunk | while | flops 551300096 | bytes 33705652 | solution.py:118
  286.9 2.9 fusion.61
  289.8 3.3 fusion.63
  293.3 3.3 fusion.65
  298.6 2.9 fusion.61
  301.4 3.3 fusion.63
  304.9 3.7 fusion.65
  310.6 2.9 fusion.61
  313.4 3.3 fusion.63
  316.9 3.7 fusion.65
  322.5 2.9 fusion.61
  325.4 3.3 fusion.63
  328.9 3.7 fusion.65
  332.6 2.1 divide_convert_fusion
  334.8 26.1 %all-gather.18.cloned.1.call-done = bf16[2048,1152]{1,0:T(8,128)(2,1)} async-done(((bf16[512,1152]{1,0:T(8,128)(2,1)}), bf16[2048,1152]{1,0:T(8,128)(2,1)}) %all-gather.18.cloned.1.call-update) | async-done | bytes 4718608 | tf_op jit(solution)/shard_map/all_gather | solution.py:130
  360.8 22.5 %all-gather.16.cloned.1.call-done = bf16[512,2048]{0,1:T(8,128)(2,1)} async-done(((bf16[512,512]{0,1:T(8,128)(2,1)}), bf16[512,2048]{0,1:T(8,128)(2,1)}) %all-gather.16.cloned.1.call-update) | async-done | bytes 2097168 | tf_op jit(solution)/shard_map/all_gather | solution.py:126
  383.3 6.9 %fusion.34 = bf16[512,1152]{1,0:T(8,128)(2,1)} fusion(bf16[512,2048]{0,1:T(8,128)(2,1)} %all-gather.16.cloned.1.call-done, bf16[2048,1152]{1,0:T(8,128)(2,1)} %all-gather.18.cloned.1.call-done, bf16[512,1152]{1,0:T(8,128)(2,1)S(1)} %copy-done.1), kind=kOutput, calls=%fused_computation.44 | convolution fusion | flops 2417688576 | bytes 9175040 | tf_op jit(solution)/shard_map/dot_general | solution.py:128
  (87 shorter events, 20.6 us)
Async XLA Ops:
  6.5 42.6 %all-gather.8.cloned.1.call-start = ((), (), s32[]{:S(2)}) async-start(), calls=%async_computation | async-start | bytes 5898240 | tf_op jit(solution)/shard_map/all_gather | solution.py:43
  6.5 94.6 %copy-start.5 = (f32[4608]{0:T(1024)S(1)}, f32[4608]{0:T(1024)}, u32[]{:S(2)}) copy-start(f32[4608]{0:T(1024)} %param.10) | copy-start | bytes 55300
  7.3 93.9 %all-gather.10.cloned.1.call-start = ((), (), s32[]{:S(2)}) async-start(), calls=%async_computation.1 | async-start | bytes 2949120 | tf_op jit(solution)/shard_map/all_gather | solution.py:48
  8.0 144.1 %all-gather.12.cloned.1.call-start = ((), (), s32[]{:S(2)}) async-start(), calls=%async_computation.2 | async-start | bytes 2949120 | tf_op jit(solution)/shard_map/all_gather | solution.py:49
  8.7 259.4 %all-gather.14.cloned.1.call-start = ((), (), s32[]{:S(2)}) async-start(), calls=%async_computation.3 | async-start | bytes 5898240 | tf_op jit(solution)/shard_map/all_gather | solution.py:47
  9.3 351.5 %all-gather.18.cloned.1.call-start = ((), (), s32[]{:S(2)}) async-start(), calls=%async_computation.5 | async-start | bytes 5898240 | tf_op jit(solution)/shard_map/all_gather | solution.py:130
  106.3 86.1 %copy-start.3 = (s32[512]{0:T(512)S(1)}, s32[512]{0:T(512)}, u32[]{:S(2)}) copy-start(s32[512]{0:T(512)} %param.15) | copy-start | bytes 6148
  156.7 22.1 %collective-permute-start = (bf16[2,512,256]{2,1,0:T(8,128)(2,1)S(1)}, bf16[2,512,256]{2,1,0:T(8,128)(2,1)S(1)}, u32[]{:S(2)}, u32[]{:S(2)}) collective-permute-start(bf16[2,512,256]{2,1,0:T(8,128)(2,1)S(1)} %pad_maximum_fusion), channel_id=1, source_target_pairs={{0,4},{4,8},{8,12},{1,5},{5,9},{9,13},{2,6},{6,10},{10,14},{3,7},{... | collective-permute-start | bytes 1572872 | tf_op jit(solution)/shard_map/ppermute | solution.py:16
  178.9 60.8 %collective-permute-start.1 = (bf16[2,512,256]{2,1,0:T(8,128)(2,1)S(1)}, bf16[2,512,256]{2,1,0:T(8,128)(2,1)S(1)}, u32[]{:S(2)}, u32[]{:S(2)}) collective-permute-start(bf16[2,512,256]{2,1,0:T(8,128)(2,1)S(1)} %collective-permute-done), channel_id=1, source_target_pairs={{0,4},{4,8},{8,12},{1,5},{5,9},{9,13},{2,6},{6,10},{10,14},{3,7},{... | collective-permute-start | bytes 1572872 | tf_op jit(solution)/shard_map/ppermute | solution.py:16
  192.3 191.0 %all-gather.16.cloned.1.call-start = ((), (), s32[]{:S(2)}) async-start(), calls=%async_computation.4 | async-start | bytes 2621440 | tf_op jit(solution)/shard_map/all_gather | solution.py:126
  239.6 36.5 %collective-permute-start.2 = (bf16[2,512,256]{2,1,0:T(8,128)(2,1)S(1)}, bf16[2,512,256]{2,1,0:T(8,128)(2,1)}, u32[]{:S(2)}, u32[]{:S(2)}) collective-permute-start(bf16[2,512,256]{2,1,0:T(8,128)(2,1)S(1)} %collective-permute-done.1), channel_id=1, source_target_pairs={{0,4},{4,8},{8,12},{1,5},{5,9},{9,13},{2,6},{6,10},{10,14},{3,7},{... | collective-permute-start | bytes 1572872 | tf_op jit(solution)/shard_map/ppermute | solution.py:16
  279.0 5.8 %copy-start.2 = (f32[512,2,2]{0,2,1:T(2,128)S(1)}, f32[512,2,2]{0,2,1:T(2,128)}, u32[]{:S(2)}) copy-start(f32[512,2,2]{0,2,1:T(2,128)} %custom-call.1) | copy-start | bytes 24580
  279.1 5.8 %copy-start.4 = (s32[512]{0:T(512)S(1)}, s32[512]{0:T(512)}, u32[]{:S(2)}) copy-start(s32[512]{0:T(512)} %param.15) | copy-start | bytes 6148
  284.8 98.5 %copy-start.1 = (bf16[512,1152]{1,0:T(8,128)(2,1)S(1)}, bf16[512,1152]{1,0:T(8,128)(2,1)}, u32[]{:S(2)}) copy-start(bf16[512,1152]{1,0:T(8,128)(2,1)} %param.9) | copy-start | bytes 3538948
  289.8 3.5 copy-start
  301.4 3.4 copy-start
  313.4 3.5 copy-start
  325.4 3.5 copy-start
Sparse Core Ops, SparseCore 0:
  8.9 40.1 all-gather.7
  50.7 50.4 all-gather.9
  102.8 49.2 all-gather.11
  153.5 114.6 all-gather.13
  269.6 91.2 all-gather.17
  362.3 21.0 all-gather.15
where the time goes:
time: 398 us; the launch traced here: 397 us
  waiting for transfers between devices  231 us (58%)
  matrix products  49.1 us (12%)
  blocking collectives  45.2 us (11%)
  other arithmetic  27.5 us (7%)
  starting transfers between devices  17.5 us (4%)
  between operations  13.7 us (3%)
  local copies, waits for them, and re-layouts  12.9 us (3%)
    all_gather x1, waiting for transfers between devices, per_device(): lax.all_gather(key_weight, 'seq', axis=0, tiled=True)  48.7 us
    all_gather x1, waiting for transfers between devices, per_device(): lax.all_gather(value_weight, 'seq', axis=0, tiled=True)  45.8 us
    all_gather x1, blocking collectives, per_device(): all_places = lax.all_gather(positions, 'seq', axis=0, tiled=True)  45.2 us
    all_gather x1, waiting for transfers between devices, per_device(): whole = lax.all_gather(tokens, 'col', axis=1, tiled=True)  38.5 us
    all_gather x1, waiting for transfers between devices, per_device(): lax.all_gather(query_weight, 'seq', axis=0, tiled=True)  26.4 us
    all_gather x1, waiting for transfers between devices, per_device(): lax.all_gather(out_weight, 'seq', axis=0, tiled=True)  26.1 us
    all_gather x1, waiting for transfers between devices, per_device(): mixed = lax.all_gather(attended, 'col', axis=1, tiled=True)  22.5 us
    ppermute x3, waiting for transfers between devices, passed_along(): return lax.ppermute(block, axis, route)  20.3 us
  transfers between devices with their start and end apart: 9, of which 7 were waited for; matrix products, arithmetic and copies ran while one was open for 21% of the time, Pallas kernels for 0%

commit v1 on v0

--- a/solution.py
+++ b/solution.py
@@ -1,3 +1,4 @@
+import functools
 import jax
 import jax.numpy as jnp
 from jax import lax
@@ -8,6 +9,27 @@
 WIN = 4096
 score_scale = 1.0 / 12.0
 rope_base = 10000.0
+
+
+def expand_the_pipes(local_values, along_dim):
+    finding = lax.axis_size("seq")
+    prior = lax.axis_index("seq")
+    everything, back = (finding, prior)
+    far_arr, top = (local_values, 1)
+    while top < everything:
+        response = lax.ppermute(
+            far_arr,
+            axis_name="seq",
+            perm=list(map(lambda num: (num, num ^ top), range(everything))),
+        )
+        tile_out = jnp.concatenate([far_arr, response], axis=along_dim)
+        w2 = jnp.concatenate([response, far_arr], axis=along_dim)
+        far_arr = jnp.where(back & top == 0, tile_out, w2)
+        top = 2 * top
+    return far_arr
+
+
+take_regions_here = functools.partial(expand_the_pipes, along_dim=0)
 
 
 def passed_along(block, axis, distance):
@@ -46,7 +68,7 @@
     pieces = (
         lax.all_gather(query_weight, "seq", axis=0, tiled=True),
         lax.all_gather(key_weight, "seq", axis=0, tiled=True),
-        lax.all_gather(value_weight, "seq", axis=0, tiled=True),
+        take_regions_here(value_weight),
     )
     columns = normed
     query_raw, key_raw, value_raw = tuple(

time: 398 us -> 367 us (0.922)
  waiting for transfers between devices: 231 us -> 190 us
  starting transfers between devices: 17.5 us -> 26.5 us
    all_gather x1 -> x0, waiting for transfers between devices: 45.8 us -> none  [per_device(): lax.all_gather(value_weight, 'seq', axis=0, tiled=True)]
    all_gather x1, waiting for transfers between devices: 38.5 us -> 19.3 us  [per_device(): whole = lax.all_gather(tokens, 'col', axis=1, tiled=True)]
    all_gather x1, waiting for transfers between devices: 48.7 us -> 66.9 us  [per_device(): lax.all_gather(key_weight, 'seq', axis=0, tiled=True)]
    ppermute x0 -> x2, waiting for transfers between devices: none -> 12.3 us  [expand_the_pipes(): lax.ppermute(far_arr, axis_name='seq', perm=list(map(lambda num: (num, nu...]
    all_gather x1, waiting for transfers between devices: 26.4 us -> 19.3 us  [per_device(): lax.all_gather(query_weight, 'seq', axis=0, tiled=True)]
    ppermute x0 -> x2, starting transfers between devices: none -> 5.9 us  [expand_the_pipes(): lax.ppermute(far_arr, axis_name='seq', perm=list(map(lambda num: (num, nu...]
  transfers between devices with their start and end apart: 9 -> 10, of which waited for: 7 -> 7; matrix products, arithmetic and copies ran while one was open for 21% -> 23% of each run, Pallas kernels for 0% -> 0%
where the time goes in v1:
time: 367 us; the launch traced here: 366 us
  waiting for transfers between devices  190 us (52%)
  matrix products  49.5 us (13%)
  blocking collectives  44.5 us (12%)
  other arithmetic  29.1 us (8%)
  starting transfers between devices  26.5 us (7%)
  between operations  13.4 us (4%)
  local copies, waits for them, and re-layouts  13 us (4%)
    all_gather x1, waiting for transfers between devices, per_device(): lax.all_gather(key_weight, 'seq', axis=0, tiled=True)  66.9 us
    all_gather x1, blocking collectives, per_device(): all_places = lax.all_gather(positions, 'seq', axis=0, tiled=True)  44.5 us
    all_gather x1, waiting for transfers between devices, per_device(): lax.all_gather(out_weight, 'seq', axis=0, tiled=True)  24.5 us
    ppermute x3, waiting for transfers between devices, passed_along(): return lax.ppermute(block, axis, route)  23.2 us
    all_gather x1, waiting for transfers between devices, per_device(): mixed = lax.all_gather(attended, 'col', axis=1, tiled=True)  22.5 us
    ppermute x3, starting transfers between devices, passed_along(): return lax.ppermute(block, axis, route)  20.4 us
    all_gather x1, waiting for transfers between devices, per_device(): whole = lax.all_gather(tokens, 'col', axis=1, tiled=True)  19.3 us
    all_gather x1, waiting for transfers between devices, per_device(): lax.all_gather(query_weight, 'seq', axis=0, tiled=True)  19.3 us
  transfers between devices with their start and end apart: 10, of which 7 were waited for; matrix products, arithmetic and copies ran while one was open for 23% of the time, Pallas kernels for 0%

profile of v1, /device:TPU:0, one launch (start us, length us, event | category | flops | bytes accessed | tf_op | source)
XLA Modules:
  0.0 366.0 jit_solution(17215651380463235871)
XLA Ops:
  8.8 3.1 collective-permute-start
  13.1 12.3 %collective-permute-done = bf16[1152,256]{1,0:T(8,128)(2,1)S(1)} collective-permute-done((bf16[1152,256]{1,0:T(8,128)(2,1)}, bf16[1152,256]{1,0:T(8,128)(2,1)S(1)}, u32[]{:S(2)}, u32[]{:S(2)}) %collective-permute-start) | collective-permute-done | bytes 589856 | tf_op jit(solution)/shard_map/ppermute | solution.py:20
  27.0 2.8 collective-permute-start.1
  29.8 19.3 %all-gather.7.cloned.1.call-done = bf16[512,4608]{1,0:T(8,128)(2,1)} async-done(((bf16[512,1152]{1,0:T(8,128)(2,1)}), bf16[512,4608]{1,0:T(8,128)(2,1)}) %all-gather.7.cloned.1.call-update) | async-done | bytes 4718608 | tf_op jit(solution)/shard_map/all_gather | solution.py:65
  49.1 3.3 fusion.31
  52.4 66.9 %all-gather.9.cloned.1.call-done = bf16[4608,256]{1,0:T(8,128)(2,1)} async-done(((bf16[1152,256]{1,0:T(8,128)(2,1)}), bf16[4608,256]{1,0:T(8,128)(2,1)}) %all-gather.9.cloned.1.call-update) | async-done | bytes 2359312 | tf_op jit(solution)/shard_map/all_gather | solution.py:70
  119.3 4.8 %fusion.48 = f32[512,256]{0,1:T(8,128)S(1)} fusion(bf16[4608,256]{1,0:T(8,128)(2,1)} %all-gather.9.cloned.1.call-done, bf16[512,4608]{1,0:T(8,128)(2,1)} %all-gather.7.cloned.1.call-done, f32[4608]{0:T(1024)S(1)} %copy-done.5, f32[512]{0:T(512)S(1)} %add_rsqrt_fusion), kind=kOutput, calls=%fused_computation.74 | convolution fusion | flops 1217396736 | bytes 7622656 | tf_op jit(solution)/shard_map/dot_general | solution.py:75
  124.4 4.9 %fusion.43 = bf16[1,512,256]{2,1,0:T(8,128)(2,1)S(1)} fusion(bf16[2304,256]{1,0:T(8,128)(2,1)} %collective-permute-done.1, bf16[2304,256]{1,0:T(8,128)(2,1)S(1)} %maximum_select_fusion.4, pred[]{:T(512)S(6)} %eq.13, bf16[512,4608]{1,0:T(8,128)(2,1)} %all-gather.7.cloned.1.call-done, f32[4608]{0:T(1024)S(1)} %copy-done.5, f32[512]{0:T(512)S(1)} %add_rsqrt_fusion), kind=kOutput, calls=%fused_computation.56 | convolution fusion | flops 1228144640 | bytes 7360513 | tf_op jit(solution)/shard_map/dot_general | solution.py:75
  130.8 23.2 %collective-permute-done.2 = bf16[2,512,256]{2,1,0:T(8,128)(2,1)S(1)} collective-permute-done((bf16[2,512,256]{2,1,0:T(8,128)(2,1)S(1)}, bf16[2,512,256]{2,1,0:T(8,128)(2,1)S(1)}, u32[]{:S(2)}, u32[]{:S(2)}) %collective-permute-start.2) | collective-permute-done | bytes 524320 | tf_op jit(solution)/shard_map/ppermute | solution.py:38
  153.9 14.2 %collective-permute-start.3 = (bf16[2,512,256]{2,1,0:T(8,128)(2,1)S(1)}, bf16[2,512,256]{2,1,0:T(8,128)(2,1)S(1)}, u32[]{:S(2)}, u32[]{:S(2)}) collective-permute-start(bf16[2,512,256]{2,1,0:T(8,128)(2,1)S(1)} %collective-permute-done.2), channel_id=1, source_target_pairs={{0,4},{4,8},{8,12},{1,5},{5,9},{9,13},{2,6},{6,10},{10,14},{3,7},{... | collective-permute-start | bytes 1572872 | tf_op jit(solution)/shard_map/ppermute | solution.py:38
  168.2 44.5 %all-gather = s32[4,1,512]{2,1,0:T(1,128)S(1)} all-gather(s32[1,1,512]{2,1,0:T(1,128)S(1)} %bitcast.74), channel_id=1, replica_groups=mesh['grp'=2,'seq'=4,'col'=4] {'seq'}, dimensions={0}, use_global_device_ids=true | all-gather | bytes 10240 | tf_op jit(solution)/shard_map/all_gather | solution.py:67
  214.7 4.9 %collective-permute-start.4 = (bf16[2,512,256]{2,1,0:T(8,128)(2,1)S(1)}, bf16[2,512,256]{2,1,0:T(8,128)(2,1)}, u32[]{:S(2)}, u32[]{:S(2)}) collective-permute-start(bf16[2,512,256]{2,1,0:T(8,128)(2,1)S(1)} %collective-permute-done.3), channel_id=1, source_target_pairs={{0,4},{4,8},{8,12},{1,5},{5,9},{9,13},{2,6},{6,10},{10,14},{3,7},{... | collective-permute-start | bytes 1572872 | tf_op jit(solution)/shard_map/ppermute | solution.py:38
  219.6 19.3 %all-gather.11.cloned.1.call-done = bf16[4608,512]{1,0:T(8,128)(2,1)} async-done(((bf16[1152,512]{1,0:T(8,128)(2,1)}), bf16[4608,512]{1,0:T(8,128)(2,1)}) %all-gather.11.cloned.1.call-update) | async-done | bytes 4718608 | tf_op jit(solution)/shard_map/all_gather | solution.py:69
  238.9 6.9 %fusion.45 = f32[512,512]{0,1:T(8,128)S(1)} fusion(bf16[4608,512]{1,0:T(8,128)(2,1)} %all-gather.11.cloned.1.call-done, bf16[512,4608]{1,0:T(8,128)(2,1)} %all-gather.7.cloned.1.call-done, f32[4608]{0:T(1024)S(1)} %copy-done.5, f32[512]{0:T(512)S(1)} %add_rsqrt_fusion), kind=kOutput, calls=%fused_computation.73 | convolution fusion | flops 2425356288 | bytes 10506240 | tf_op jit(solution)/shard_map/dot_general | solution.py:75
  253.3 2.3 rev.15
  255.6 47.9 %while.15 = (s32[]{:T(128)}, f32[512,2,2]{0,2,1:T(2,128)S(1)}, f32[512,2,2]{0,2,1:T(2,128)S(1)}, f32[512,2,2,128]{0,3,2,1:T(8,128)}, s32[4,512]{1,0:T(4,128)}, /...) while((s32[]{:T(128)}, f32[512,2,2]{0,2,1:T(2,128)S(1)}, ...), condition=%wide.region_4.5_spmd.clone, body=%wide.region_1.4_spmd.clone.sunk | while | flops 551300096 | bytes 33705652 | solution.py:140
  257.7 2.9 fusion.69
  260.5 3.3 fusion.71
  264.1 3.3 fusion.73
  269.4 2.9 fusion.69
  272.2 3.3 fusion.71
  275.7 3.7 %fusion.73 = f32[512,2,2,128]{0,3,2,1:T(8,128)} fusion(f32[2,512,512,2]{2,1,3,0:T(8,128)S(1)} %copy-done, f32[512,2,2]{0,2,1:T(2,128)S(1)} %fusion.70, pred[512,512]{0,1:T(8,128)(4,1)S(1)} %fusion.68, f32[512,2,2,128]{0,3,2,1:T(8,128)} %get-tuple-element.235, f32[512,2,2]{0,2,1:T(2,128)S(1)} %get-tuple-element.218, pred[]{:T(512)S(6)} %compare.4, ...), kind=kOutput, calls=%fused_computation.15.clone.1 | convolution fusion | flops 273416192 | bytes 6832641 | tf_op jit(solution)/shard_map/while/body/eval_jaxpr/qgek,kgh->qgeh/dot_general | solution.py:127
  281.4 2.9 fusion.69
  284.3 3.3 fusion.71
  287.8 3.7 %fusion.73 = f32[512,2,2,128]{0,3,2,1:T(8,128)} fusion(f32[2,512,512,2]{2,1,3,0:T(8,128)S(1)} %copy-done, f32[512,2,2]{0,2,1:T(2,128)S(1)} %fusion.70, pred[512,512]{0,1:T(8,128)(4,1)S(1)} %fusion.68, f32[512,2,2,128]{0,3,2,1:T(8,128)} %get-tuple-element.235, f32[512,2,2]{0,2,1:T(2,128)S(1)} %get-tuple-element.218, pred[]{:T(512)S(6)} %compare.4, ...), kind=kOutput, calls=%fused_computation.15.clone.1 | convolution fusion | flops 273416192 | bytes 6832641 | tf_op jit(solution)/shard_map/while/body/eval_jaxpr/qgek,kgh->qgeh/dot_general | solution.py:127
  293.4 2.9 fusion.69
  296.3 3.3 fusion.71
  299.8 3.7 %fusion.73 = f32[512,2,2,128]{0,3,2,1:T(8,128)} fusion(f32[2,512,512,2]{2,1,3,0:T(8,128)S(1)} %copy-done, f32[512,2,2]{0,2,1:T(2,128)S(1)} %fusion.70, pred[512,512]{0,1:T(8,128)(4,1)S(1)} %fusion.68, f32[512,2,2,128]{0,3,2,1:T(8,128)} %get-tuple-element.235, f32[512,2,2]{0,2,1:T(2,128)S(1)} %get-tuple-element.218, pred[]{:T(512)S(6)} %compare.4, ...), kind=kOutput, calls=%fused_computation.15.clone.1 | convolution fusion | flops 273416192 | bytes 6832641 | tf_op jit(solution)/shard_map/while/body/eval_jaxpr/qgek,kgh->qgeh/dot_general | solution.py:127
  303.5 2.1 divide_convert_fusion
  305.6 24.5 %all-gather.15.cloned.1.call-done = bf16[2048,1152]{1,0:T(8,128)(2,1)} async-done(((bf16[512,1152]{1,0:T(8,128)(2,1)}), bf16[2048,1152]{1,0:T(8,128)(2,1)}) %all-gather.15.cloned.1.call-update) | async-done | bytes 4718608 | tf_op jit(solution)/shard_map/all_gather | solution.py:152
  330.1 22.5 %all-gather.13.cloned.1.call-done = bf16[512,2048]{0,1:T(8,128)(2,1)} async-done(((bf16[512,512]{0,1:T(8,128)(2,1)}), bf16[512,2048]{0,1:T(8,128)(2,1)}) %all-gather.13.cloned.1.call-update) | async-done | bytes 2097168 | tf_op jit(solution)/shard_map/all_gather | solution.py:148
  352.6 6.9 %fusion.34 = bf16[512,1152]{1,0:T(8,128)(2,1)} fusion(bf16[512,2048]{0,1:T(8,128)(2,1)} %all-gather.13.cloned.1.call-done, bf16[2048,1152]{1,0:T(8,128)(2,1)} %all-gather.15.cloned.1.call-done, bf16[512,1152]{1,0:T(8,128)(2,1)S(1)} %copy-done.1), kind=kOutput, calls=%fused_computation.44 | convolution fusion | flops 2417688576 | bytes 9175040 | tf_op jit(solution)/shard_map/dot_general | solution.py:150
  (89 shorter events, 24.9 us)
Async XLA Ops:
  6.5 42.6 %all-gather.7.cloned.1.call-start = ((), (), s32[]{:S(2)}) async-start(), calls=%async_computation | async-start | bytes 5898240 | tf_op jit(solution)/shard_map/all_gather | solution.py:65
  7.3 112.0 %all-gather.9.cloned.1.call-start = ((), (), s32[]{:S(2)}) async-start(), calls=%async_computation.1 | async-start | bytes 2949120 | tf_op jit(solution)/shard_map/all_gather | solution.py:70
  8.0 111.3 %copy-start.5 = (f32[4608]{0:T(1024)S(1)}, f32[4608]{0:T(1024)}, u32[]{:S(2)}) copy-start(f32[4608]{0:T(1024)} %param.10) | copy-start | bytes 55300
  8.0 230.9 %all-gather.11.cloned.1.call-start = ((), (), s32[]{:S(2)}) async-start(), calls=%async_computation.2 | async-start | bytes 5898240 | tf_op jit(solution)/shard_map/all_gather | solution.py:69
  8.8 321.3 %all-gather.15.cloned.1.call-start = ((), (), s32[]{:S(2)}) async-start(), calls=%async_computation.4 | async-start | bytes 5898240 | tf_op jit(solution)/shard_map/all_gather | solution.py:152
  8.8 16.6 %collective-permute-start = (bf16[1152,256]{1,0:T(8,128)(2,1)}, bf16[1152,256]{1,0:T(8,128)(2,1)S(1)}, u32[]{:S(2)}, u32[]{:S(2)}) collective-permute-start(bf16[1152,256]{1,0:T(8,128)(2,1)} %param.13), channel_id=1, source_target_pairs={{0,4},{4,0},{8,12},{12,8},{1,5},{5,1},{9,13},{13,9},{2,6},{6,2},{1... | collective-permute-start | bytes 1769480 | tf_op jit(solution)/shard_map/ppermute | solution.py:20
  27.0 97.4 %collective-permute-start.1 = (bf16[2304,256]{1,0:T(8,128)(2,1)S(1)}, bf16[2304,256]{1,0:T(8,128)(2,1)}, u32[]{:S(2)}, u32[]{:S(2)}) collective-permute-start(bf16[2304,256]{1,0:T(8,128)(2,1)S(1)} %maximum_select_fusion.4), channel_id=1, source_target_pairs={{0,8},{4,12},{8,0},{12,4},{1,9},{5,13},{9,1},{13,5},{2,10},{6,14},... | collective-permute-start | bytes 3538952 | tf_op jit(solution)/shard_map/ppermute | solution.py:20
  124.4 43.8 %copy-start.3 = (s32[512]{0:T(512)S(1)}, s32[512]{0:T(512)}, u32[]{:S(2)}) copy-start(s32[512]{0:T(512)} %param.15) | copy-start | bytes 6148
  129.4 24.5 %collective-permute-start.2 = (bf16[2,512,256]{2,1,0:T(8,128)(2,1)S(1)}, bf16[2,512,256]{2,1,0:T(8,128)(2,1)S(1)}, u32[]{:S(2)}, u32[]{:S(2)}) collective-permute-start(bf16[2,512,256]{2,1,0:T(8,128)(2,1)S(1)} %pad_maximum_fusion), channel_id=1, source_target_pairs={{0,4},{4,8},{8,12},{1,5},{5,9},{9,13},{2,6},{6,10},{10,14},{3,7},{... | collective-permute-start | bytes 1572872 | tf_op jit(solution)/shard_map/ppermute | solution.py:38
  153.9 60.8 %collective-permute-start.3 = (bf16[2,512,256]{2,1,0:T(8,128)(2,1)S(1)}, bf16[2,512,256]{2,1,0:T(8,128)(2,1)S(1)}, u32[]{:S(2)}, u32[]{:S(2)}) collective-permute-start(bf16[2,512,256]{2,1,0:T(8,128)(2,1)S(1)} %collective-permute-done.2), channel_id=1, source_target_pairs={{0,4},{4,8},{8,12},{1,5},{5,9},{9,13},{2,6},{6,10},{10,14},{3,7},{... | collective-permute-start | bytes 1572872 | tf_op jit(solution)/shard_map/ppermute | solution.py:38
  168.1 184.4 %all-gather.13.cloned.1.call-start = ((), (), s32[]{:S(2)}) async-start(), calls=%async_computation.3 | async-start | bytes 2621440 | tf_op jit(solution)/shard_map/all_gather | solution.py:148
  214.7 32.1 %collective-permute-start.4 = (bf16[2,512,256]{2,1,0:T(8,128)(2,1)S(1)}, bf16[2,512,256]{2,1,0:T(8,128)(2,1)}, u32[]{:S(2)}, u32[]{:S(2)}) collective-permute-start(bf16[2,512,256]{2,1,0:T(8,128)(2,1)S(1)} %collective-permute-done.3), channel_id=1, source_target_pairs={{0,4},{4,8},{8,12},{1,5},{5,9},{9,13},{2,6},{6,10},{10,14},{3,7},{... | collective-permute-start | bytes 1572872 | tf_op jit(solution)/shard_map/ppermute | solution.py:38
  249.8 5.8 %copy-start.2 = (f32[512,2,2]{0,2,1:T(2,128)S(1)}, f32[512,2,2]{0,2,1:T(2,128)}, u32[]{:S(2)}) copy-start(f32[512,2,2]{0,2,1:T(2,128)} %custom-call.1) | copy-start | bytes 24580
  249.8 5.8 %copy-start.4 = (s32[512]{0:T(512)S(1)}, s32[512]{0:T(512)}, u32[]{:S(2)}) copy-start(s32[512]{0:T(512)} %param.15) | copy-start | bytes 6148
  255.6 97.0 %copy-start.1 = (bf16[512,1152]{1,0:T(8,128)(2,1)S(1)}, bf16[512,1152]{1,0:T(8,128)(2,1)}, u32[]{:S(2)}) copy-start(bf16[512,1152]{1,0:T(8,128)(2,1)} %param.9) | copy-start | bytes 3538948
  260.5 3.5 copy-start
  272.2 3.5 copy-start
  284.3 3.5 copy-start
  296.3 3.5 copy-start
Sparse Core Ops, SparseCore 0:
  8.9 40.1 all-gather.6
  50.7 68.6 all-gather.8
  120.9 117.9 all-gather.10
  240.3 89.7 all-gather.14
  331.5 21.0 all-gather.12
